TPU v7x, 256 devices: a whole 4x4x8 slice. The times are simulated.
256 devices in a mesh: span: 8 (over x_lo, y), seq: 32 (over x_hi, z, core).
Axes of the slice: x: 4 (x_hi: 2, x_lo: 2; x = x_hi * 2 + x_lo), y: 4, z: 8, core: 2. Of those that a mesh axis runs over, the one named last changes fastest.
Arguments:
- noisy_qkv: bfloat16 [8, 1280, 3, 4096], P('span', 'seq'), may hold values from -20 to 20
- clean_cache: bfloat16 [8, 1280, 2, 4096], P('span', 'seq'), may hold values from -6 to 6
- span_ids: int32 [8], P('span'), may hold values from 0 to 7, each once
- sign_bits: int32 [128], replicated, may hold values 0 or 1
Outputs:
- attended: bfloat16 [8, 1280, 4096], P('span', 'seq')
All inputs are finite; a program needn't handle non-finite values.
Results may differ from a plain program's by a relative error of at most 0.007.
Values may be sent and summed in bfloat16 or wider, within the bound.
A program may use at most 128 MiB of HBM per device.

v0:
```python
import math

import jax
import jax.numpy as jnp
from jax import lax
from jax.sharding import PartitionSpec as P

HD = 128


def hadamard_table(extent):
    row_index = lax.broadcasted_iota(jnp.int32, (extent, extent), 0)
    col_index = lax.broadcasted_iota(jnp.int32, (extent, extent), 1)
    parity = jnp.zeros((extent, extent), jnp.int32)
    for digit in range(extent.bit_length() - 1):
        parity = parity + row_index // 2**digit % 2 * (col_index // 2**digit % 2)
    return (1 - 2 * (parity % 2)).astype(jnp.float32)


def turn_back(stored, hadamard, sign_scale):
    return (
        jnp.einsum("...d,de->...e", stored, hadamard, precision=lax.Precision.HIGHEST) * sign_scale
    )


def per_device(noisy_qkv, clean_cache, span_ids, sign_bits):
    hadamard = hadamard_table(HD)
    sign_scale = (2 * sign_bits - 1).astype(jnp.float32) / math.sqrt(HD)
    score_scale = 1.0 / math.sqrt(HD)
    my_id = span_ids[0]
    spread = lax.all_to_all(noisy_qkv, "seq", split_axis=3, concat_axis=1, tiled=True)
    length = spread.shape[1]
    heads_local = spread.shape[3] // HD
    pieces = spread[0].reshape(length, 3, heads_local, HD)
    queries = pieces[:, 0]
    own_keys = pieces[:, 1]
    own_values = pieces[:, 2]
    scores = (
        jnp.einsum("qhd,khd->hqk", queries, own_keys, preferred_element_type=jnp.float32)
        * score_scale
    )
    row_max = jnp.max(scores, axis=-1)
    weights = jnp.exp(scores - row_max[..., None])
    row_sum = jnp.sum(weights, axis=-1)
    near_acc = jnp.einsum(
        "hqk,khd->hqd", weights.astype(jnp.bfloat16), own_values, preferred_element_type=jnp.float32
    )
    state = (row_max, row_sum, near_acc, jnp.zeros_like(near_acc))
    query_side = jnp.einsum(
        "qhd,de->hqe",
        queries.astype(jnp.float32) * sign_scale,
        hadamard,
        precision=lax.Precision.HIGHEST,
    ).astype(jnp.bfloat16)

    def absorb_tile(running, cached):
        old_max, old_sum, near_now, far_now = running
        scores = (
            jnp.einsum("hqd,khd->hqk", query_side, cached[:, 0], preferred_element_type=jnp.float32)
            * score_scale
        )
        new_max = jnp.maximum(old_max, jnp.max(scores, axis=-1))
        factor = jnp.exp(old_max - new_max)
        weights = jnp.exp(scores - new_max[..., None])
        new_sum = old_sum * factor + jnp.sum(weights, axis=-1)
        rounded = weights.astype(jnp.bfloat16)
        far_now = far_now * factor[..., None] + jnp.einsum(
            "hqk,khd->hqd", rounded, cached[:, 1], preferred_element_type=jnp.float32
        )
        near_now = near_now * factor[..., None]
        return (new_max, new_sum, near_now, far_now)

    stacked, seen_ids = (
        lax.all_gather(clean_cache, "span", axis=0, tiled=True),
        lax.all_gather(span_ids, "span", axis=0, tiled=True),
    )
    head_cache = lax.all_to_all(stacked, "seq", split_axis=3, concat_axis=1, tiled=True)
    running = state

    def visit(carried, entry):
        cached, seen_id = entry
        cached = cached.reshape(cached.shape[0], 2, heads_local, HD)
        visible = seen_id < my_id
        updated = absorb_tile(carried, cached)
        carried = jax.tree.map(
            lambda fresh, older: jnp.where(visible, fresh, older), updated, carried
        )
        return (carried, None)

    running, _ = lax.scan(visit, running, (head_cache, seen_ids))
    state = running
    final_max, final_sum, near_acc, far_acc = state
    near_acc = near_acc + turn_back(far_acc, hadamard, sign_scale)
    result = near_acc / final_sum[..., None]
    mixed = (
        jnp.transpose(result, (1, 0, 2)).reshape(1, length, heads_local * HD).astype(jnp.bfloat16)
    )
    return lax.all_to_all(mixed, "seq", split_axis=1, concat_axis=2, tiled=True)


def solution(mesh):
    placed = (P("span", "seq", None, None), P("span", "seq", None, None), P("span"), P())
    return jax.shard_map(
        per_device, mesh=mesh, in_specs=placed, out_specs=P("span", "seq", None), check_vma=False
    )
```

profile of v0, /device:TPU:1, one launch (start us, length us, event | category | flops | bytes accessed | tf_op | source)
XLA Modules:
  0.0 465.6 jit_solution(10356920412477131913)
XLA Ops:
  6.5 2.3 copy.38
  8.9 6.1 %copy.36 = bf16[1,40,3,4096]{1,2,0,3:T(4,128)(2,1)} copy(bf16[1,40,3,4096]{3,1,2,0:T(8,128)(2,1)} %param.6) | data formatting | bytes 1966080 | tf_op args[0]
  14.9 8.2 %reshape.101 = bf16[32,2,7680]{2,1,0:T(2,128)(2,1)} reshape(bf16[4096,1,3,40]{3,2,1,0:T(4,128)(2,1)} %bitcast.95) | data formatting | bytes 1966080
  23.2 12.6 %all-to-all-start = ((bf16[32,2,7680]{2,1,0:T(2,128)(2,1)}), bf16[32,2,7680]{2,1,0:T(2,128)(2,1)S(1)}, u32[]{:S(2)}, u32[]{:S(2)}) async-start(bf16[32,2,7680]{2,1,0:T(2,128)(2,1)} %reshape.101), calls=%async_computation | async-start | bytes 1966080 | tf_op jit(solution)/shard_map/all_to_all | solution.py:31
  35.8 52.7 %all-gather.2.cloned.1.call-done = bf16[8,40,2,4096]{3,1,2,0:T(8,128)(2,1)} async-done(((bf16[1,40,2,4096]{3,1,2,0:T(8,128)(2,1)}), bf16[8,40,2,4096]{3,1,2,0:T(8,128)(2,1)}) %all-gather.2.cloned.1.call-update) | async-done | bytes 5242896 | tf_op jit(solution)/shard_map/all_gather | solution.py:74
  88.5 18.8 %copy.39 = bf16[8,40,2,4096]{1,0,2,3:T(8,128)(2,1)} copy(bf16[8,40,2,4096]{3,1,2,0:T(8,128)(2,1)} %all-gather.2.cloned.1.call-done) | data formatting | bytes 10485760 | tf_op jit(solution)/shard_map/all_gather | solution.py:74
  107.3 31.9 %reshape.103 = bf16[32,2,40960]{2,1,0:T(2,128)(2,1)} reshape(bf16[4096,2,8,40]{3,2,1,0:T(8,128)(2,1)} %bitcast.92) | data formatting | bytes 10485760
  139.2 10.2 %all-to-all-start.1 = ((bf16[32,2,40960]{2,1,0:T(2,128)(2,1)}), bf16[32,2,40960]{2,1,0:T(2,128)(2,1)}, u32[]{:S(2)}, u32[]{:S(2)}) async-start(bf16[32,2,40960]{2,1,0:T(2,128)(2,1)} %reshape.103), calls=%async_computation.1 | async-start | bytes 10485760 | tf_op jit(solution)/shard_map/all_to_all | solution.py:77
  151.3 7.7 %all-reduce = s32[8]{0:T(128)S(1)} all-reduce(s32[8]{0:T(128)S(1)} %dynamic-update-slice), channel_id=1, replica_groups=mesh['span'=8,'seq'=32] {'span'}, use_global_device_ids=true, to_apply=%add | all-reduce | flops 8 | bytes 64
  159.2 6.5 %reshape.102 = bf16[4096,1,3,40]{3,2,1,0:T(4,128)(2,1)} reshape(bf16[32,2,7680]{2,1,0:T(2,128)(2,1)S(1)} %all-to-all-done) | data formatting | bytes 1966080
  165.6 5.5 %copy.37 = bf16[1,40,3,32,128]{4,1,3,2,0:T(8,128)(2,1)S(1)} copy(bf16[1,40,3,32,128]{1,2,4,3,0:T(4,128)(2,1)} %bitcast.94) | data formatting | bytes 1966080 | tf_op jit(solution)/shard_map/all_to_all | solution.py:31
  171.2 1.1 fusion.29
  172.5 1.0 fusion.79
  173.6 1.0 fusion.18
  174.6 1.1 fusion.25
  175.7 92.2 %all-to-all-done.1 = bf16[32,2,40960]{2,1,0:T(2,128)(2,1)} async-done(((bf16[32,2,40960]{2,1,0:T(2,128)(2,1)}), bf16[32,2,40960]{2,1,0:T(2,128)(2,1)}, u32[]{:S(2)}, u32[]{:S(2)}) %all-to-all-start.1) | async-done | bytes 5242912 | tf_op jit(solution)/shard_map/all_to_all | solution.py:77
  267.9 32.2 %reshape.104 = bf16[4096,2,8,40]{3,2,1,0:T(8,128)(2,1)} reshape(bf16[32,2,40960]{2,1,0:T(2,128)(2,1)} %all-to-all-done.1) | data formatting | bytes 10485760
  300.1 17.7 %copy.40 = bf16[8,32,40,2,128]{4,2,1,3,0:T(8,128)(2,1)} copy(bf16[8,32,40,2,128]{2,0,3,4,1:T(8,128)(2,1)} %bitcast.93) | data formatting | bytes 10485760 | tf_op jit(solution)/shard_map/all_to_all | solution.py:77
  317.8 102.9 %while.17 = (s32[]{:T(128)}, f32[1,1280]{1,0:T(1,128)S(1)}, f32[1,1280]{1,0:T(1,128)S(1)}, f32[1,1280,128]{2,1,0:T(8,128)S(1)}, f32[1,1280,128]{2,1,0:T(8,128)S(...) while((s32[]{:T(128)}, f32[1,1280]{1,0:T(1,128)S(1)}, ...), condition=%wide.region_5.6_spmd.clone, body=%wide.region_2.5_spmd.clone.sunk | while | flops 849681920 | bytes 50878632 | solution.py:90
  317.8 1.1 dynamic-slice_bitcast_fusion.2
  318.9 3.8 fusion.86
  324.7 4.7 %fusion.89 = f32[1,1280,128]{2,1,0:T(8,128)S(1)} fusion(f32[1280,1280]{1,0:T(8,128)} %get-tuple-element.246, f32[1280]{0:T(1024)S(1)} %get-tuple-element.248, f32[1,1280,128]{2,1,0:T(8,128)S(1)} %get-tuple-element.267, bf16[1280,2,1,128]{3,0,2,1:T(8,128)(2,1)S(1)} %dynamic-slice_bitcast_fusion.2, f32[1280]{0:T(1024)S(1)} %get-tuple-element.251, ...), kind=kOutput, calls=%fused_computation.8.clone.1 | convolution fusion | flops 423362560 | bytes 8208386 | tf_op jit(solution)/shard_map/while/body/eval_jaxpr/hqk,khd->hqd/dot_general | solution.py:67
  329.4 1.0 fusion.88
  330.7 1.1 dynamic-slice_bitcast_fusion.2
  331.8 3.8 fusion.86
  337.5 4.7 %fusion.89 = f32[1,1280,128]{2,1,0:T(8,128)S(1)} fusion(f32[1280,1280]{1,0:T(8,128)} %get-tuple-element.246, f32[1280]{0:T(1024)S(1)} %get-tuple-element.248, f32[1,1280,128]{2,1,0:T(8,128)S(1)} %get-tuple-element.267, bf16[1280,2,1,128]{3,0,2,1:T(8,128)(2,1)S(1)} %dynamic-slice_bitcast_fusion.2, f32[1280]{0:T(1024)S(1)} %get-tuple-element.251, ...), kind=kOutput, calls=%fused_computation.8.clone.1 | convolution fusion | flops 423362560 | bytes 8208386 | tf_op jit(solution)/shard_map/while/body/eval_jaxpr/hqk,khd->hqd/dot_general | solution.py:67
  343.6 1.1 dynamic-slice_bitcast_fusion.2
  344.7 3.8 fusion.86
  350.4 4.7 %fusion.89 = f32[1,1280,128]{2,1,0:T(8,128)S(1)} fusion(f32[1280,1280]{1,0:T(8,128)} %get-tuple-element.246, f32[1280]{0:T(1024)S(1)} %get-tuple-element.248, f32[1,1280,128]{2,1,0:T(8,128)S(1)} %get-tuple-element.267, bf16[1280,2,1,128]{3,0,2,1:T(8,128)(2,1)S(1)} %dynamic-slice_bitcast_fusion.2, f32[1280]{0:T(1024)S(1)} %get-tuple-element.251, ...), kind=kOutput, calls=%fused_computation.8.clone.1 | convolution fusion | flops 423362560 | bytes 8208386 | tf_op jit(solution)/shard_map/while/body/eval_jaxpr/hqk,khd->hqd/dot_general | solution.py:67
  356.4 1.1 dynamic-slice_bitcast_fusion.2
  357.6 3.8 fusion.86
  363.3 4.7 %fusion.89 = f32[1,1280,128]{2,1,0:T(8,128)S(1)} fusion(f32[1280,1280]{1,0:T(8,128)} %get-tuple-element.246, f32[1280]{0:T(1024)S(1)} %get-tuple-element.248, f32[1,1280,128]{2,1,0:T(8,128)S(1)} %get-tuple-element.267, bf16[1280,2,1,128]{3,0,2,1:T(8,128)(2,1)S(1)} %dynamic-slice_bitcast_fusion.2, f32[1280]{0:T(1024)S(1)} %get-tuple-element.251, ...), kind=kOutput, calls=%fused_computation.8.clone.1 | convolution fusion | flops 423362560 | bytes 8208386 | tf_op jit(solution)/shard_map/while/body/eval_jaxpr/hqk,khd->hqd/dot_general | solution.py:67
  369.3 1.1 dynamic-slice_bitcast_fusion.2
  370.4 3.8 fusion.86
  376.1 4.7 %fusion.89 = f32[1,1280,128]{2,1,0:T(8,128)S(1)} fusion(f32[1280,1280]{1,0:T(8,128)} %get-tuple-element.246, f32[1280]{0:T(1024)S(1)} %get-tuple-element.248, f32[1,1280,128]{2,1,0:T(8,128)S(1)} %get-tuple-element.267, bf16[1280,2,1,128]{3,0,2,1:T(8,128)(2,1)S(1)} %dynamic-slice_bitcast_fusion.2, f32[1280]{0:T(1024)S(1)} %get-tuple-element.251, ...), kind=kOutput, calls=%fused_computation.8.clone.1 | convolution fusion | flops 423362560 | bytes 8208386 | tf_op jit(solution)/shard_map/while/body/eval_jaxpr/hqk,khd->hqd/dot_general | solution.py:67
  382.2 1.1 dynamic-slice_bitcast_fusion.2
  383.3 3.8 fusion.86
  389.0 4.7 %fusion.89 = f32[1,1280,128]{2,1,0:T(8,128)S(1)} fusion(f32[1280,1280]{1,0:T(8,128)} %get-tuple-element.246, f32[1280]{0:T(1024)S(1)} %get-tuple-element.248, f32[1,1280,128]{2,1,0:T(8,128)S(1)} %get-tuple-element.267, bf16[1280,2,1,128]{3,0,2,1:T(8,128)(2,1)S(1)} %dynamic-slice_bitcast_fusion.2, f32[1280]{0:T(1024)S(1)} %get-tuple-element.251, ...), kind=kOutput, calls=%fused_computation.8.clone.1 | convolution fusion | flops 423362560 | bytes 8208386 | tf_op jit(solution)/shard_map/while/body/eval_jaxpr/hqk,khd->hqd/dot_general | solution.py:67
  395.0 1.1 dynamic-slice_bitcast_fusion.2
  396.2 3.8 fusion.86
  401.9 4.7 %fusion.89 = f32[1,1280,128]{2,1,0:T(8,128)S(1)} fusion(f32[1280,1280]{1,0:T(8,128)} %get-tuple-element.246, f32[1280]{0:T(1024)S(1)} %get-tuple-element.248, f32[1,1280,128]{2,1,0:T(8,128)S(1)} %get-tuple-element.267, bf16[1280,2,1,128]{3,0,2,1:T(8,128)(2,1)S(1)} %dynamic-slice_bitcast_fusion.2, f32[1280]{0:T(1024)S(1)} %get-tuple-element.251, ...), kind=kOutput, calls=%fused_computation.8.clone.1 | convolution fusion | flops 423362560 | bytes 8208386 | tf_op jit(solution)/shard_map/while/body/eval_jaxpr/hqk,khd->hqd/dot_general | solution.py:67
  407.9 1.1 dynamic-slice_bitcast_fusion.2
  409.0 3.8 fusion.86
  414.7 4.7 %fusion.89 = f32[1,1280,128]{2,1,0:T(8,128)S(1)} fusion(f32[1280,1280]{1,0:T(8,128)} %get-tuple-element.246, f32[1280]{0:T(1024)S(1)} %get-tuple-element.248, f32[1,1280,128]{2,1,0:T(8,128)S(1)} %get-tuple-element.267, bf16[1280,2,1,128]{3,0,2,1:T(8,128)(2,1)S(1)} %dynamic-slice_bitcast_fusion.2, f32[1280]{0:T(1024)S(1)} %get-tuple-element.251, ...), kind=kOutput, calls=%fused_computation.8.clone.1 | convolution fusion | flops 423362560 | bytes 8208386 | tf_op jit(solution)/shard_map/while/body/eval_jaxpr/hqk,khd->hqd/dot_general | solution.py:67
  420.8 1.1 fusion.28
  421.9 5.3 %copy.49 = bf16[1,1280,128]{2,0,1:T(2,128)(2,1)S(1)} copy(bf16[1,1280,128]{2,1,0:T(8,128)(2,1)S(1)} %fusion.28) | data formatting | bytes 655360 | tf_op jit(solution)/shard_map/convert_element_type | solution.py:96
  427.7 7.4 %reduce.15 = bf16[1280,128]{1,0:T(8,128)(2,1)S(1)} reduce(bf16[1280,1,128]{2,1,0:T(2,128)(2,1)S(1)} %bitcast.100, bf16[]{:T(256)} %broadcast.372), dimensions={1}, to_apply=%bitcast.79.reduce_sub_computation | reduce | bytes 655362
  435.2 22.4 %all_to_all.51 = bf16[32,2,2560]{2,1,0:T(2,128)(2,1)S(1)} all-to-all(bf16[32,2,2560]{2,1,0:T(2,128)(2,1)S(1)} %reshape.105), channel_id=1, replica_groups=mesh['span'=8,'seq'=32] {'seq'}, dimensions={0} | all-to-all | bytes 655360 | tf_op jit(solution)/shard_map/all_to_all | solution.py:98
  (85 shorter events, 18.0 us)
Async XLA Ops:
  6.5 82.0 %all-gather.2.cloned.1.call-start = ((), (), s32[]{:S(2)}) async-start(), calls=%async_computation.3 | async-start | bytes 5898240 | tf_op jit(solution)/shard_map/all_gather | solution.py:74
  23.2 116.0 %all-to-all-start = ((bf16[32,2,7680]{2,1,0:T(2,128)(2,1)}), bf16[32,2,7680]{2,1,0:T(2,128)(2,1)S(1)}, u32[]{:S(2)}, u32[]{:S(2)}) async-start(bf16[32,2,7680]{2,1,0:T(2,128)(2,1)} %reshape.101), calls=%async_computation | async-start | bytes 1966080 | tf_op jit(solution)/shard_map/all_to_all | solution.py:31
  139.2 10.8 %copy-start.2 = (u32[256]{0:T(256)S(1)}, u32[256]{0:T(256)}, u32[]{:S(2)}) copy-start(u32[256]{0:T(256)} %constant.266) | copy-start | bytes 3076
  139.2 20.0 %copy-start.1 = (s32[128]{0:T(128)S(1)}, s32[128]{0:T(128)}, u32[]{:S(2)}) copy-start(s32[128]{0:T(128)} %param.9) | copy-start | bytes 1540
  139.2 128.7 %all-to-all-start.1 = ((bf16[32,2,40960]{2,1,0:T(2,128)(2,1)}), bf16[32,2,40960]{2,1,0:T(2,128)(2,1)}, u32[]{:S(2)}, u32[]{:S(2)}) async-start(bf16[32,2,40960]{2,1,0:T(2,128)(2,1)} %reshape.103), calls=%async_computation.1 | async-start | bytes 10485760 | tf_op jit(solution)/shard_map/all_to_all | solution.py:77
  324.6 4.7 %copy-start = (f32[1280,1280]{1,0:T(8,128)S(1)}, f32[1280,1280]{1,0:T(8,128)}, u32[]{:S(2)}) copy-start(f32[1280,1280]{1,0:T(8,128)} %get-tuple-element.246) | copy-start | bytes 19660804 | tf_op jit(solution)/shard_map/while
  337.5 4.7 %copy-start = (f32[1280,1280]{1,0:T(8,128)S(1)}, f32[1280,1280]{1,0:T(8,128)}, u32[]{:S(2)}) copy-start(f32[1280,1280]{1,0:T(8,128)} %get-tuple-element.246) | copy-start | bytes 19660804 | tf_op jit(solution)/shard_map/while
  350.4 4.7 %copy-start = (f32[1280,1280]{1,0:T(8,128)S(1)}, f32[1280,1280]{1,0:T(8,128)}, u32[]{:S(2)}) copy-start(f32[1280,1280]{1,0:T(8,128)} %get-tuple-element.246) | copy-start | bytes 19660804 | tf_op jit(solution)/shard_map/while
  363.3 4.7 %copy-start = (f32[1280,1280]{1,0:T(8,128)S(1)}, f32[1280,1280]{1,0:T(8,128)}, u32[]{:S(2)}) copy-start(f32[1280,1280]{1,0:T(8,128)} %get-tuple-element.246) | copy-start | bytes 19660804 | tf_op jit(solution)/shard_map/while
  376.1 4.7 %copy-start = (f32[1280,1280]{1,0:T(8,128)S(1)}, f32[1280,1280]{1,0:T(8,128)}, u32[]{:S(2)}) copy-start(f32[1280,1280]{1,0:T(8,128)} %get-tuple-element.246) | copy-start | bytes 19660804 | tf_op jit(solution)/shard_map/while
  389.0 4.7 %copy-start = (f32[1280,1280]{1,0:T(8,128)S(1)}, f32[1280,1280]{1,0:T(8,128)}, u32[]{:S(2)}) copy-start(f32[1280,1280]{1,0:T(8,128)} %get-tuple-element.246) | copy-start | bytes 19660804 | tf_op jit(solution)/shard_map/while
  401.9 4.7 %copy-start = (f32[1280,1280]{1,0:T(8,128)S(1)}, f32[1280,1280]{1,0:T(8,128)}, u32[]{:S(2)}) copy-start(f32[1280,1280]{1,0:T(8,128)} %get-tuple-element.246) | copy-start | bytes 19660804 | tf_op jit(solution)/shard_map/while
  414.7 4.7 %copy-start = (f32[1280,1280]{1,0:T(8,128)S(1)}, f32[1280,1280]{1,0:T(8,128)}, u32[]{:S(2)}) copy-start(f32[1280,1280]{1,0:T(8,128)} %get-tuple-element.246) | copy-start | bytes 19660804 | tf_op jit(solution)/shard_map/while
Sparse Core Ops, SparseCore 0:
  9.1 79.3 all-gather.1
where the time goes:
time: 469 us; the launch traced here: 466 us
  local copies, waits for them, and re-layouts  152 us (32%)
  waiting for transfers between devices  145 us (31%)
  matrix products  71.9 us (15%)
  blocking collectives  30.1 us (6%)
  starting transfers between devices  22.7 us (5%)
  other arithmetic  18.9 us (4%)
  between operations  14.2 us (3%)
  loops' own time  10.7 us (2%)
    all_to_all x1, waiting for transfers between devices, per_device(): lax.all_to_all(stacked, 'seq', split_axis=3, concat_axis=1, tiled=True)  92.2 us
    unnamed x18, local copies, waits for them, and re-layouts  89.7 us
    all_gather x1, waiting for transfers between devices, per_device(): lax.all_gather(clean_cache, 'span', axis=0, tiled=True)  52.7 us
    dot_general x8, matrix products, absorb_tile(): jnp.einsum('hqk,khd->hqd', rounded, cached[:, 1], preferred_element_type=...  37.5 us
    dot_general x8, matrix products, absorb_tile(): jnp.einsum('hqd,khd->hqk', query_side, cached[:, 0], preferred_element_ty...  30 us
    all_to_all x1, blocking collectives, per_device(): return lax.all_to_all(mixed, 'seq', split_axis=1, concat_axis=2, tiled=True)  22.4 us
    all_gather x1, local copies, waits for them, and re-layouts, per_device(): lax.all_gather(clean_cache, 'span', axis=0, tiled=True)  18.8 us
    all_to_all x1, local copies, waits for them, and re-layouts, per_device(): lax.all_to_all(stacked, 'seq', split_axis=3, concat_axis=1, tiled=True)  17.7 us
  transfers between devices with their start and end apart: 3, of which 2 were waited for; matrix products, arithmetic and copies ran while one was open for 18% of the time, Pallas kernels for 0%

commit v1 on v0

v1 whole, which is shorter than its diff:
```python
import math

import jax
import jax.numpy as jnp
from jax import lax
from jax.experimental import pallas as pl
from jax.experimental.pallas import tpu as pltpu
from jax.sharding import PartitionSpec as P

HD = 128
ROW = 8
LOG2E_SCALE = math.log2(math.e) / math.sqrt(HD)
HIDDEN = -1e30
OFF = 1e30
F32 = jnp.float32
BF16 = jnp.bfloat16


def turn_matrix(sign_row):
    row = lax.broadcasted_iota(jnp.int32, (HD, HD), 0)
    col = lax.broadcasted_iota(jnp.int32, (HD, HD), 1)
    both = row & col
    parity = jnp.zeros((HD, HD), jnp.int32)
    for digit in range(HD.bit_length() - 1):
        parity = parity + ((both >> digit) & 1)
    entry = 1 - 2 * (parity & 1)
    return (entry * (2 * sign_row - 1)).astype(F32).astype(BF16)


def make_kernel(n_span, n_seq, tiles, x_size):
    ring = n_span // x_size
    unit = n_seq * tiles
    tokens = unit * ROW
    n_chunk = 4
    chunk = tokens // n_chunk
    own = n_span
    per_chunk = n_seq // n_chunk

    def kernel(
        sign_ref, id_ref, cache_ref, noisy_ref, out_ref,
        kv, qraw, sides, key_s, val_s, m_s, l_s, a_s, outbuf,
        in_send, in_recv, local_sem, ring_send, ring_recv, out_send, out_recv,
    ):
        span = lax.axis_index("span")
        seq = lax.axis_index("seq")
        x = span // ring
        y = span % ring
        x_other = (x + 1) % x_size
        up, down = (y + 1) % ring, (y + ring - 1) % ring
        partner = x_other * ring + y
        above, below = x * ring + up, x * ring + down
        far_above, far_below = x_other * ring + up, x_other * ring + down

        barrier = pltpu.get_barrier_semaphore()

        def greet(k, carry):
            t = lax.rem(seq + k, n_seq)
            pl.semaphore_signal(barrier, inc=1, device_id=(span, t))
            return carry

        lax.fori_loop(1, n_seq, greet, 0)
        for target in (partner, above, below):
            pl.semaphore_signal(barrier, inc=1, device_id=(target, seq))
        pl.semaphore_wait(barrier, n_seq - 1 + 3)

        mine = pl.ds(seq * tiles, tiles)

        def columns(t):
            return pl.ds(pl.multiple_of(t * HD, HD), HD)

        def scatter(src, dst, which):
            def send(k, carry):
                t = lax.rem(seq + k, n_seq)
                pltpu.make_async_remote_copy(
                    src_ref=src.at[:, :, columns(t)],
                    dst_ref=dst.at[mine],
                    send_sem=in_send.at[which],
                    recv_sem=in_recv.at[which],
                    device_id=(span, t),
                ).start()
                return carry

            lax.fori_loop(1, n_seq, send, 0)
            pltpu.make_async_copy(src.at[:, :, columns(seq)], dst.at[mine], in_recv.at[which]).start()

        def scattered(dst, which):
            whole = dst.at[pl.ds(0, unit)]
            pltpu.make_async_copy(whole, whole, in_recv.at[which]).wait()

        def unit_of(kind, j):
            return kv.at[kind, j, pl.ds(0, unit + 1 - kind)]

        def pass_on(kind, j, target, slot):
            pltpu.make_async_remote_copy(
                src_ref=unit_of(kind, j),
                dst_ref=unit_of(kind, j),
                send_sem=ring_send.at[slot],
                recv_sem=ring_recv.at[kind, j],
                device_id=(target, seq),
            ).start()

        def sent(kind, j, slot):
            whole = unit_of(kind, j)
            pltpu.make_async_copy(whole, whole, ring_send.at[slot]).wait()

        def arrived(kind, j):
            whole = unit_of(kind, j)
            pltpu.make_async_copy(whole, whole, ring_recv.at[kind, j]).wait()

        scatter(cache_ref.at[0], kv.at[0, span], 0)
        scatter(cache_ref.at[1], kv.at[1, span], 1)

        my_id = jnp.full((ROW, HD), id_ref[0], jnp.int32).astype(F32)
        kv[0, span, unit] = my_id.astype(BF16)
        kv[0, own, unit] = jnp.full((ROW, HD), -1.0, F32).astype(BF16)
        m_s[...] = jnp.full(m_s.shape, HIDDEN, F32)
        l_s[...] = jnp.zeros(l_s.shape, F32)
        a_s[...] = jnp.zeros(a_s.shape, F32)
        val_s[:, HD:] = jnp.ones((tokens, HD), BF16)
        turn = turn_matrix(sign_ref[...])

        scattered(kv.at[0, span], 0)
        pass_on(0, span, above, 0)
        pass_on(0, span, below, 1)
        pass_on(0, span, partner, 2)
        scatter(noisy_ref.at[0], qraw, 2)
        scattered(kv.at[1, span], 1)
        pass_on(1, span, above, 3)
        pass_on(1, span, below, 4)
        pass_on(1, span, partner, 5)
        scatter(noisy_ref.at[1], kv.at[0, own], 3)
        scatter(noisy_ref.at[2], kv.at[1, own], 4)
        arrived(0, partner)
        pass_on(0, partner, above, 6)
        pass_on(0, partner, below, 7)
        arrived(1, partner)
        pass_on(1, partner, above, 8)
        pass_on(1, partner, below, 9)
        arrived(0, below)
        pass_on(0, below, above, 10)
        arrived(1, above)
        pass_on(1, above, below, 11)

        scattered(qraw, 2)
        query = qraw[...].astype(F32).reshape(tokens, HD).astype(BF16)
        sides[1] = query
        sides[0] = (
            lax.dot_general(query, turn, (((1,), (1,)), ((), ())), preferred_element_type=F32)
            * (1.0 / math.sqrt(HD))
        ).astype(BF16)

        def dense(kind, j):
            return kv[kind, j, pl.ds(0, unit)].astype(F32).reshape(tokens, HD).astype(BF16)

        opposite = (y + 2) % ring
        order = (
            partner, above, below, far_above, own, far_below,
            x * ring + opposite, x_other * ring + opposite,
        )
        near_step = 4

        def step(i, carry):
            j = order[0]
            for place in range(1, len(order)):
                j = jnp.where(i == place, order[place], j)
            side = jnp.where(i == near_step, 1, 0)

            @pl.when(i == 2)
            def _():
                arrived(0, far_below)
                pass_on(0, far_below, above, 12)

            @pl.when(i == 3)
            def _():
                arrived(1, far_above)
                pass_on(1, far_above, below, 13)

            @pl.when(i == near_step)
            def _():
                scattered(kv.at[0, own], 3)
                scattered(kv.at[1, own], 4)

            @pl.when((i == 1) | (i == 3) | (i > 5))
            def _():
                arrived(0, j)

            @pl.when((i == 2) | (i > 4))
            def _():
                arrived(1, j)

            key_s[...] = dense(0, j)
            val_s[:, :HD] = dense(1, j)
            seen = (kv[0, j, unit].astype(F32) < my_id)[:1, :1]

            for c in range(n_chunk):
                rows = pl.ds(c * chunk, chunk)
                scores = lax.dot_general(
                    sides[side, rows], key_s[...], (((1,), (1,)), ((), ())),
                    preferred_element_type=F32,
                )
                top = jnp.max(scores, axis=1, keepdims=True) * LOG2E_SCALE
                top = jnp.where(seen, top, HIDDEN)
                old = m_s[side, rows][:, :1]
                new = jnp.maximum(old, top)
                weights = jnp.exp2(scores * LOG2E_SCALE - jnp.where(seen, new, OFF)).astype(BF16)
                factor = jnp.exp2(old - new)
                part = jnp.dot(weights, val_s[...], preferred_element_type=F32)
                l_s[side, rows] = l_s[side, rows] * factor + part[:, HD:]
                a_s[side, rows] = a_s[side, rows] * factor + part[:, :HD]
                m_s[side, rows] = jnp.broadcast_to(new, (chunk, HD))
            return carry

        lax.fori_loop(0, len(order), step, 0)

        def finish(k, carry):
            c = lax.rem(k + seq // per_chunk, n_chunk)
            rows = pl.ds(pl.multiple_of(c * chunk, chunk), chunk)
            best = jnp.maximum(m_s[0, rows], m_s[1, rows])
            far_factor = jnp.exp2(m_s[0, rows] - best)
            near_factor = jnp.exp2(m_s[1, rows] - best)
            far = a_s[0, rows]
            high = far.astype(BF16)
            low = (far - high.astype(F32)).astype(BF16)
            turned = (
                jnp.dot(high, turn, preferred_element_type=F32)
                + jnp.dot(low, turn, preferred_element_type=F32)
            ) * (1.0 / math.sqrt(HD))
            total = l_s[0, rows] * far_factor + l_s[1, rows] * near_factor
            result = (a_s[1, rows] * near_factor + turned * far_factor) / total
            outbuf[pl.ds(c * per_chunk * tiles, per_chunk * tiles)] = (
                result.reshape(per_chunk * tiles, ROW, HD).astype(BF16)
            )

            def give(u, inner):
                t = c * per_chunk + u
                piece = outbuf.at[pl.ds(t * tiles, tiles)]
                place = out_ref.at[:, :, columns(seq)]

                @pl.when(t != seq)
                def _():
                    pltpu.make_async_remote_copy(
                        src_ref=piece, dst_ref=place, send_sem=out_send, recv_sem=out_recv,
                        device_id=(span, t),
                    ).start()

                @pl.when(t == seq)
                def _():
                    pltpu.make_async_copy(piece, place, out_recv).start()

                return inner

            lax.fori_loop(0, per_chunk, give, 0)
            return carry

        lax.fori_loop(0, n_chunk, finish, 0)

        others = kv.at[0, 0, pl.ds(0, (n_seq - 1) * tiles)]
        for which in range(5):
            pltpu.make_async_copy(others, others, in_send.at[which]).wait()
        for slot, (kind, j) in enumerate(
            [(0, span)] * 3 + [(1, span)] * 3 + [(0, partner)] * 2 + [(1, partner)] * 2
            + [(0, below), (1, above), (0, far_below), (1, far_above)]
        ):
            sent(kind, j, slot)
        pltpu.make_async_copy(others, others, out_send).wait()
        pltpu.make_async_copy(outbuf, outbuf, out_recv).wait()

    return kernel


def per_device(noisy_qkv, clean_cache, span_ids, sign_bits):
    n_span, n_seq = lax.axis_size("span"), lax.axis_size("seq")
    _, rows, _, width = noisy_qkv.shape
    tiles = rows // ROW
    unit = n_seq * tiles
    tokens = unit * ROW
    noisy = jnp.transpose(noisy_qkv[0], (1, 0, 2)).reshape(3, tiles, ROW, width)
    cache = jnp.transpose(clean_cache[0], (1, 0, 2)).reshape(2, tiles, ROW, width)
    vmem, anywhere = pl.BlockSpec(memory_space=pltpu.VMEM), pl.BlockSpec(memory_space=pl.ANY)
    smem = pl.BlockSpec(memory_space=pltpu.SMEM)
    dma = pltpu.SemaphoreType.DMA
    out = pl.pallas_call(
        make_kernel(n_span, n_seq, tiles, 2),
        out_shape=jax.ShapeDtypeStruct((tiles, ROW, width), BF16),
        in_specs=[vmem, smem, anywhere, anywhere],
        out_specs=anywhere,
        scratch_shapes=[
            pltpu.VMEM((2, n_span + 1, unit + 1, ROW, HD), BF16),
            pltpu.VMEM((unit, ROW, HD), BF16),
            pltpu.VMEM((2, tokens, HD), BF16),
            pltpu.VMEM((tokens, HD), BF16),
            pltpu.VMEM((tokens, 2 * HD), BF16),
            pltpu.VMEM((2, tokens, HD), F32),
            pltpu.VMEM((2, tokens, HD), F32),
            pltpu.VMEM((2, tokens, HD), F32),
            pltpu.VMEM((unit, ROW, HD), BF16),
            dma((5,)), dma((5,)), dma, dma((14,)), dma((2, n_span)), dma, dma,
        ],
        compiler_params=pltpu.CompilerParams(
            collective_id=0, has_side_effects=True, vmem_limit_bytes=50 * 2**20
        ),
        cost_estimate=pl.CostEstimate(
            flops=8 * 4 * tokens * tokens * HD, bytes_accessed=2 * 2**20,
            transcendentals=8 * tokens * tokens,
        ),
        name="span_attention",
    )(sign_bits.reshape(1, HD), span_ids, cache, noisy)
    return out.reshape(1, rows, width)


def solution(mesh):
    placed = (P("span", "seq", None, None), P("span", "seq", None, None), P("span"), P())
    return jax.shard_map(
        per_device, mesh=mesh, in_specs=placed, out_specs=P("span", "seq", None), check_vma=False
    )
```

time: 469 us -> 89.7 us (0.19)
  local copies, waits for them, and re-layouts: 152 us -> 2.82 us
  waiting for transfers between devices: 145 us -> 0 us
  Pallas kernels: 0 us -> 86 us
  matrix products: 71.9 us -> 0 us
  blocking collectives: 30.1 us -> 0 us
  starting transfers between devices: 22.7 us -> 0 us
  other arithmetic: 18.9 us -> 0 us
  between operations: 14.2 us -> 0.76 us
  loops' own time: 10.7 us -> 0 us
    all_to_all x2 -> x0, waiting for transfers between devices: 92.2 us -> none  [the longest x1 92.2 us: per_device(): lax.all_to_all(stacked, 'seq', split_axis=3, concat_axis=1, tiled=True)]
    unnamed x18 -> x5, local copies, waits for them, and re-layouts: 89.7 us -> 1.37 us
    pallas_call x0 -> x1, Pallas kernels: none -> 86 us  [per_device(): pl.pallas_call(make_kernel(n_span, n_seq, tiles, 2), out_shape=jax.ShapeD...]
    dot_general x20 -> x0, matrix products: 71.9 us -> none  [the longest x8 37.5 us: absorb_tile(): jnp.einsum('hqk,khd->hqd', rounded, cached[:, 1], preferred_element_type=...]
    all_gather x1 -> x0, waiting for transfers between devices: 52.7 us -> none  [per_device(): lax.all_gather(clean_cache, 'span', axis=0, tiled=True)]
    all_to_all x3 -> x0, local copies, waits for them, and re-layouts: 24.1 us -> none  [the longest x1 17.7 us: per_device(): lax.all_to_all(stacked, 'seq', split_axis=3, concat_axis=1, tiled=True)]
    all_to_all x2 -> x0, starting transfers between devices: 22.7 us -> none  [the longest x1 12.6 us: per_device(): lax.all_to_all(noisy_qkv, 'seq', split_axis=3, concat_axis=1, tiled=True)]
    all_to_all x1 -> x0, blocking collectives: 22.4 us -> none  [per_device(): return lax.all_to_all(mixed, 'seq', split_axis=1, concat_axis=2, tiled=True)]
  transfers between devices with their start and end apart: 3 -> 0, of which waited for: 2 -> 0; matrix products, arithmetic and copies ran while one was open for 18% -> 0% of each run, Pallas kernels for 0% -> 0%
where the time goes in v1:
time: 89.7 us; the launch traced here: 89.6 us
  Pallas kernels  86 us (96%)
  local copies, waits for them, and re-layouts  2.82 us (3%)
    pallas_call x1, Pallas kernels, per_device(): pl.pallas_call(make_kernel(n_span, n_seq, tiles, 2), out_shape=jax.ShapeD...  86 us

profile of v1, /device:TPU:1, one launch (start us, length us, event | category | flops | bytes accessed | tf_op | source)
XLA Modules:
  0.0 89.6 jit_solution(4501675327641974974)
XLA Ops:
  0.0 0.0 copy-start
  0.7 1.5 %copy.7 = bf16[2,40,4096]{2,1,0:T(8,128)(2,1)S(1)} copy(bf16[2,40,4096]{2,0,1:T(2,128)(2,1)} %bitcast.17) | data formatting | bytes 1310720 | tf_op jit(solution)/shard_map/transpose | solution.py:278
  2.2 0.0 copy-start.1
  2.2 0.0 copy-done
  2.2 0.6 copy-done.1
  2.9 86.0 %span_attention.1 = bf16[5,8,4096]{2,1,0:T(8,128)(2,1)S(1)} custom-call(s32[1,128]{1,0:T(1,128)S(1)} %bitcast.16, s32[1]{0:T(128)S(6)} %copy.9.id_ref, bf16[2,5,8,4096]{3,2,1,0:T(8,128)(2,1)S(1)} %bitcast.13, bf16[3,5,8,4096]{3,2,1,0:T(8,128)(2,1)S(1)} %bitcast.15), custom_call_target="tpu_custom_call" | custom-call | flops 6710886400 | bytes 2097152 | tf_op jit(solution)/shard_map/span_attention/pallas_call | solution.py:282
  88.9 0.7 copy.10
Async XLA Ops:
  0.0 2.2 %copy-start = (bf16[1,40,3,4096]{3,1,2,0:T(8,128)(2,1)S(1)}, bf16[1,40,3,4096]{3,1,2,0:T(8,128)(2,1)}, u32[]{:S(2)}) copy-start(bf16[1,40,3,4096]{3,1,2,0:T(8,128)(2,1)} %param.4) | copy-start | bytes 2949124
  2.2 0.7 copy-start.1

commit v2 on v1

v2 whole, which is shorter than its diff:
```python
import math

import jax
import jax.numpy as jnp
from jax import lax
from jax.experimental import pallas as pl
from jax.experimental.pallas import tpu as pltpu
from jax.sharding import PartitionSpec as P

HD = 128
ROW = 8
X_SIZE = 2
N_CHUNK = 4
SPREAD = 64
LOG2E_SCALE = math.log2(math.e) / math.sqrt(HD)
HIDDEN = -1e30
OFF = 1e30
F32 = jnp.float32
BF16 = jnp.bfloat16


def turn_matrix(sign_row):
    row = lax.broadcasted_iota(jnp.int32, (HD, HD), 0)
    col = lax.broadcasted_iota(jnp.int32, (HD, HD), 1)
    both = row & col
    parity = jnp.zeros((HD, HD), jnp.int32)
    for digit in range(HD.bit_length() - 1):
        parity = parity + ((both >> digit) & 1)
    entry = 1 - 2 * (parity & 1)
    return (entry * (2 * sign_row - 1)).astype(F32).astype(BF16)


def make_kernel(n_span, n_seq, tiles, x_size):
    ring = n_span // x_size
    line = n_seq // 4
    unit = n_seq * tiles
    tokens = unit * ROW
    half_unit, half = unit // 2, tokens // 2
    n_chunk = N_CHUNK
    chunk = tokens // n_chunk
    near = ring
    per_chunk = n_seq // n_chunk
    id_rows = pl.ds(tokens, 2 * ROW)

    def kernel(
        sign_ref, id_ref, cache_ref, noisy_ref, out_ref,
        kv, qraw, sides, key_s, val_s, m_s, l_s, a_s, part_out, part_in, stat_out, stat_in, outbuf,
        in_send, in_recv, ring_send, ring_recv, x_send, x_recv, out_send, out_recv,
    ):
        span = lax.axis_index("span")
        seq = lax.axis_index("seq")
        x = span // ring
        y = span % ring
        above, below = (y + 1) % ring, (y + ring - 1) % ring
        opposite = (y + 2) % ring
        partner = ((x + 1) % x_size) * ring + y
        lane, plane = seq % 2, seq // (n_seq // 2)
        spot = seq // 2 % line
        corner = plane * 2 + lane

        def seat(distance, place):
            return place // 2 * 2 * line + lax.rem(spot + distance + line, line) * 2 + place % 2

        barrier = pltpu.get_barrier_semaphore()

        def greet(k, carry):
            pl.semaphore_signal(barrier, inc=1, device_id=(span, lax.rem(seq + k, n_seq)))
            return carry

        lax.fori_loop(1, n_seq, greet, 0)
        for target in (partner, x * ring + above, x * ring + below):
            pl.semaphore_signal(barrier, inc=1, device_id=(target, seq))
        pl.semaphore_wait(barrier, n_seq - 1 + 3)

        def columns(t):
            return pl.ds(pl.multiple_of(t * HD, HD), HD)

        def slab(first, slot):
            return pl.ds(first + slot * tiles, tiles)

        two = jnp.where(lane == 1, 2, -2)
        routes = (
            ((0, 0), (1, 8), (-1, 4), (two, 12)),
            ((4, 28), (3, 24), (-3, 20), (-two, 16)),
        )

        def scatter(src, dst, first, which, group):
            for distance, base in routes[group]:
                here = dst.at[slab(first, base + corner)]

                def send(p, carry, distance=distance, here=here):
                    t = seat(distance, lax.rem(corner + p, 4))
                    pltpu.make_async_remote_copy(
                        src_ref=src.at[:, :, columns(t)],
                        dst_ref=here,
                        send_sem=in_send.at[which, group],
                        recv_sem=in_recv.at[which, group],
                        device_id=(span, t),
                    ).start()
                    return carry

                if group == 0 and base == 0:
                    lax.fori_loop(1, 4, send, 0)
                    pltpu.make_async_copy(
                        src.at[:, :, columns(seq)], here, in_recv.at[which, group]
                    ).start()
                else:
                    lax.fori_loop(0, 4, send, 0)

        def scattered(dst, first, which, group):
            whole = dst.at[pl.ds(first + group * half_unit, half_unit)]
            pltpu.make_async_copy(whole, whole, in_recv.at[which, group]).wait()

        def unit_of(kind, j, group):
            if group == 0:
                return kv.at[kind, j, pl.ds(kind, half_unit + 1 - kind)]
            return kv.at[kind, j, pl.ds(1 + half_unit, half_unit)]

        ring_sent = []

        def pass_on(kind, j, group, target):
            pltpu.make_async_remote_copy(
                src_ref=unit_of(kind, j, group),
                dst_ref=unit_of(kind, j, group),
                send_sem=ring_send.at[len(ring_sent)],
                recv_sem=ring_recv.at[kind, j, group],
                device_id=(x * ring + target, seq),
            ).start()
            ring_sent.append((kind, j, group))

        def arrived(kind, j, group):
            whole = unit_of(kind, j, group)
            pltpu.make_async_copy(whole, whole, ring_recv.at[kind, j, group]).wait()

        def cross(src, dst, slot):
            return pltpu.make_async_remote_copy(
                src_ref=src, dst_ref=dst, send_sem=x_send.at[slot], recv_sem=x_recv.at[slot],
                device_id=(partner, seq),
            )

        queries_across = cross(sides.at[0], sides.at[2], 0)

        def rows_of(c):
            return pl.ds(c * chunk, chunk)

        parts_across = [
            cross(part_out.at[rows_of(c)], part_in.at[rows_of(c)], 1 + c) for c in range(n_chunk)
        ]
        stats_across = [
            cross(stat_out.at[c], stat_in.at[c], 1 + n_chunk + c) for c in range(n_chunk)
        ]

        scatter(cache_ref.at[0], kv.at[0, y], 1, 0, 0)
        scatter(cache_ref.at[1], kv.at[1, y], 1, 1, 0)
        scatter(noisy_ref.at[0], qraw, 0, 2, 0)
        scatter(noisy_ref.at[0], qraw, 0, 2, 1)

        my_id = jnp.full((2 * ROW, HD), id_ref[0], jnp.int32).astype(F32).astype(BF16)
        kv[0, y, 0] = my_id[:ROW]
        sides[0, id_rows] = my_id
        m_s[...] = jnp.full(m_s.shape, HIDDEN, F32)
        l_s[...] = jnp.zeros(l_s.shape, F32)
        a_s[...] = jnp.zeros(a_s.shape, F32)
        for j in range(ring + 1):
            val_s[j, :, HD:] = jnp.ones((tokens, HD), BF16)
        stat_out[...] = jnp.zeros(stat_out.shape, F32)
        turn = turn_matrix(sign_ref[...])

        scattered(kv.at[0, y], 1, 0, 0)
        pass_on(0, y, 0, above)
        pass_on(0, y, 0, below)
        scattered(kv.at[1, y], 1, 1, 0)
        pass_on(1, y, 0, above)
        pass_on(1, y, 0, below)
        scatter(cache_ref.at[0], kv.at[0, y], 1, 0, 1)
        arrived(0, below, 0)
        pass_on(0, below, 0, above)
        arrived(1, above, 0)
        pass_on(1, above, 0, below)
        scattered(qraw, 0, 2, 0)
        scattered(qraw, 0, 2, 1)
        query = qraw[...].astype(F32).reshape(tokens, HD).astype(BF16)
        sides[0, pl.ds(0, tokens)] = (
            lax.dot_general(query, turn, (((1,), (1,)), ((), ())), preferred_element_type=F32)
            * (1.0 / math.sqrt(HD))
        ).astype(BF16)
        queries_across.start()
        sides[1, pl.ds(0, tokens)] = query
        scatter(cache_ref.at[1], kv.at[1, y], 1, 1, 1)

        plan = (
            (0, above, 0), (0, below, 0), (0, opposite, 0),
            (2, y, 0), (2, above, 0), (2, below, 0), (2, opposite, 0),
            (2, y, 1), (2, above, 1), (2, below, 1), (2, opposite, 1),
            (0, above, 1), (0, below, 1), (0, opposite, 1),
        )

        def pick(i, field):
            got = plan[0][field]
            for place in range(1, len(plan)):
                got = jnp.where(i == place, plan[place][field], got)
            return got

        diagonal = lax.broadcasted_iota(jnp.int32, (SPREAD, HD), 0) == lax.broadcasted_iota(
            jnp.int32, (SPREAD, HD), 1
        )

        def loosen(j, group, size, count):
            rows = pl.ds(pl.multiple_of(group * half, half), size)
            for kind, dst in ((0, key_s), (1, val_s)):
                dst[j, rows, :HD] = (
                    kv[kind, j, pl.ds(1 + group * half_unit, count)]
                    .astype(F32).reshape(size, HD).astype(BF16)
                )

        def score(side, rows, keys):
            return lax.dot_general(
                sides[side, rows], keys, (((1,), (1,)), ((), ())), preferred_element_type=F32
            )

        def absorb(state, side, j, group, order, after):
            seen = (kv[0, j, 0].astype(F32) < sides[side, id_rows].astype(F32)[:ROW])[:1, :1]
            here = pl.ds(pl.multiple_of(group * half, half), half)
            ahead = score(side, rows_of(order[0]), key_s[j, here])
            for place, c in enumerate(order):
                rows = rows_of(c)
                scores = ahead
                if place + 1 < n_chunk:
                    ahead = score(side, rows_of(order[place + 1]), key_s[j, here])
                top = jnp.max(scores, axis=1, keepdims=True) * LOG2E_SCALE
                top = jnp.where(seen, top, HIDDEN)
                old = m_s[state, rows][:, :1]
                new = jnp.maximum(old, top)
                weights = jnp.exp2(scores * LOG2E_SCALE - jnp.where(seen, new, OFF)).astype(BF16)
                factor = jnp.exp2(old - new)
                part = jnp.dot(weights, val_s[j, here], preferred_element_type=F32)
                l_s[state, rows] = l_s[state, rows] * factor + part[:, HD:]
                a_s[state, rows] = a_s[state, rows] * factor + part[:, :HD]
                m_s[state, rows] = jnp.broadcast_to(new, (chunk, HD))
                after(c)

        def step(i, carry):
            side, j, group = pick(i, 0), pick(i, 1), pick(i, 2)

            @pl.when(i == 0)
            def _():
                arrived(0, above, 0)

            @pl.when(i == 1)
            def _():
                arrived(1, below, 0)

            @pl.when(i == 2)
            def _():
                arrived(0, opposite, 0)
                arrived(1, opposite, 0)

            @pl.when(i == 3)
            def _():
                scattered(kv.at[0, y], 1, 0, 1)
                pass_on(0, y, 1, above)
                pass_on(0, y, 1, below)
                for group in range(2):
                    scatter(noisy_ref.at[1], kv.at[0, near], 1, 3, group)
                queries_across.wait_recv()

            @pl.when(i == 6)
            def _():
                scattered(kv.at[1, y], 1, 1, 1)
                pass_on(1, y, 1, above)
                pass_on(1, y, 1, below)
                for group in range(2):
                    scatter(noisy_ref.at[2], kv.at[1, near], 1, 4, group)

            @pl.when(i == 7)
            def _():
                arrived(0, below, 1)
                pass_on(0, below, 1, above)

            @pl.when(i == 8)
            def _():
                arrived(1, above, 1)
                pass_on(1, above, 1, below)
                arrived(0, above, 1)

            @pl.when(i == 9)
            def _():
                arrived(1, below, 1)

            @pl.when((i < 4) | (i > 6))
            def _():
                loosen(j, group, half, half_unit)

            absorb(side // 2, side, j, group, tuple(range(n_chunk)), lambda c: None)
            return carry

        lax.fori_loop(0, 10, step, 0)

        arrived(0, opposite, 1)
        arrived(1, opposite, 1)
        loosen(opposite, 1, half, half_unit)

        def give_part(c):
            part_out[rows_of(c)] = a_s[1, rows_of(c)].astype(BF16)
            for b in range(chunk // SPREAD):
                rows = pl.ds(c * chunk + b * SPREAD, SPREAD)
                for place, stat in ((0, m_s), (ROW, l_s)):
                    stat_out[c, pl.ds(place + b, 1)] = jnp.sum(
                        jnp.where(diagonal, stat[1, rows], 0.0), axis=0, keepdims=True
                    )
            parts_across[c].start()
            stats_across[c].start()

        backward = tuple(reversed(range(n_chunk)))
        absorb(1, 2, opposite, 1, backward, give_part)

        def own_step(i, carry):
            absorb(0, 0, pick(i, 1), 1, tuple(range(n_chunk)), lambda c: None)
            return carry

        lax.fori_loop(11, len(plan), own_step, 0)

        for which in (3, 4):
            for group in range(2):
                scattered(kv.at[which - 3, near], 1, which, group)
        loosen(near, 0, tokens, unit)
        place = out_ref.at[:, :, columns(seq)]

        def give(slot, t):
            pltpu.make_async_remote_copy(
                src_ref=outbuf.at[slab(0, slot)], dst_ref=place,
                send_sem=out_send, recv_sem=out_recv, device_id=(span, t),
            ).start()

        back = ((0, 0), (1, 1), (-1, -1), (2, -2), (-2, 2), (3, 3), (-3, -3), (4, 4))
        ahead = score(1, pl.ds((n_chunk - 1) * chunk, chunk), key_s[near])
        for c in backward:
            rows = rows_of(c)
            scores = ahead
            if c > 0:
                ahead = score(1, pl.ds((c - 1) * chunk, chunk), key_s[near])
            top = jnp.max(scores, axis=1, keepdims=True) * LOG2E_SCALE
            weights = jnp.exp2(scores * LOG2E_SCALE - top).astype(BF16)
            part = jnp.dot(weights, val_s[near], preferred_element_type=F32)
            parts_across[c].wait_recv()
            stats_across[c].wait_recv()
            for b in range(chunk // SPREAD):
                some = pl.ds(c * chunk + b * SPREAD, SPREAD)
                for start, stat in ((0, m_s), (ROW, l_s)):
                    spread = jnp.broadcast_to(stat_in[c, pl.ds(start + b, 1)], (SPREAD, HD))
                    stat[1, some] = jnp.broadcast_to(
                        jnp.sum(jnp.where(diagonal, spread, 0.0), axis=1, keepdims=True),
                        (SPREAD, HD),
                    )
            best = jnp.maximum(jnp.maximum(m_s[0, rows], m_s[1, rows]), top)
            far_factor = jnp.exp2(m_s[0, rows] - best)
            near_factor = jnp.exp2(top - best)
            across_factor = jnp.exp2(m_s[1, rows] - best)
            far = a_s[0, rows] * far_factor + part_in[rows].astype(F32) * across_factor
            high = far.astype(BF16)
            low = (far - high.astype(F32)).astype(BF16)
            turned = (
                jnp.dot(high, turn, preferred_element_type=F32)
                + jnp.dot(low, turn, preferred_element_type=F32)
            ) * (1.0 / math.sqrt(HD))
            total = (
                l_s[0, rows] * far_factor + part[:, HD:] * near_factor + l_s[1, rows] * across_factor
            )
            result = (part[:, :HD] * near_factor + turned) / total
            outbuf[pl.ds(c * per_chunk * tiles, per_chunk * tiles)] = (
                result.reshape(per_chunk * tiles, ROW, HD).astype(BF16)
            )
            for g in reversed(range(2 * c, 2 * c + 2)):
                for p in range(4):
                    if g > 0:
                        give(4 * g + p, seat(back[g][p % 2], p))
                    elif p > 0:
                        other = lax.rem(corner + p, 4)
                        give(other, seat(0, other))
        own_copy = pltpu.make_async_copy(outbuf.at[slab(0, corner)], place, out_recv)
        own_copy.start()

        def drained(count, sem):
            some = outbuf.at[pl.ds(0, count * tiles)]
            pltpu.make_async_copy(some, some, sem).wait()

        for which in range(5):
            drained(n_seq // 2 - 1, in_send.at[which, 0])
            drained(n_seq // 2, in_send.at[which, 1])
        for slot, (kind, j, group) in enumerate(ring_sent):
            whole = unit_of(kind, j, group)
            pltpu.make_async_copy(whole, whole, ring_send.at[slot]).wait()
        for copy in [queries_across] + parts_across + stats_across:
            copy.wait_send()
        drained(n_seq - 1, out_send)
        drained(n_seq, out_recv)

    return kernel


def per_device(noisy_qkv, clean_cache, span_ids, sign_bits):
    n_span, n_seq = lax.axis_size("span"), lax.axis_size("seq")
    _, rows, _, width = noisy_qkv.shape
    tiles = rows // ROW
    unit = n_seq * tiles
    tokens = unit * ROW
    ring = n_span // X_SIZE
    noisy = jnp.transpose(noisy_qkv[0], (1, 0, 2)).reshape(3, tiles, ROW, width)
    cache = jnp.transpose(clean_cache[0], (1, 0, 2)).reshape(2, tiles, ROW, width)
    vmem, anywhere = pl.BlockSpec(memory_space=pltpu.VMEM), pl.BlockSpec(memory_space=pl.ANY)
    smem = pl.BlockSpec(memory_space=pltpu.SMEM)
    dma = pltpu.SemaphoreType.DMA
    out = pl.pallas_call(
        make_kernel(n_span, n_seq, tiles, X_SIZE),
        out_shape=jax.ShapeDtypeStruct((tiles, ROW, width), BF16),
        in_specs=[vmem, smem, anywhere, anywhere],
        out_specs=anywhere,
        scratch_shapes=[
            pltpu.VMEM((2, ring + 1, unit + 1, ROW, HD), BF16),
            pltpu.VMEM((unit, ROW, HD), BF16),
            pltpu.VMEM((3, tokens + 2 * ROW, HD), BF16),
            pltpu.VMEM((ring + 1, tokens, HD), BF16),
            pltpu.VMEM((ring + 1, tokens, 2 * HD), BF16),
            pltpu.VMEM((2, tokens, HD), F32),
            pltpu.VMEM((2, tokens, HD), F32),
            pltpu.VMEM((2, tokens, HD), F32),
            pltpu.VMEM((tokens, HD), BF16),
            pltpu.VMEM((tokens, HD), BF16),
            pltpu.VMEM((N_CHUNK, 2 * ROW, HD), F32),
            pltpu.VMEM((N_CHUNK, 2 * ROW, HD), F32),
            pltpu.VMEM((unit, ROW, HD), BF16),
            dma((5, 2)), dma((5, 2)), dma((12,)), dma((2, ring, 2)),
            dma((2 * N_CHUNK + 1,)), dma((2 * N_CHUNK + 1,)), dma, dma,
        ],
        compiler_params=pltpu.CompilerParams(
            collective_id=0, has_side_effects=True, vmem_limit_bytes=50 * 2**20
        ),
        cost_estimate=pl.CostEstimate(
            flops=8 * 4 * tokens * tokens * HD, bytes_accessed=2 * 2**20,
            transcendentals=8 * tokens * tokens,
        ),
        name="span_attention",
    )(sign_bits.reshape(1, HD), span_ids, cache, noisy)
    return out.reshape(1, rows, width)


def solution(mesh):
    placed = (P("span", "seq", None, None), P("span", "seq", None, None), P("span"), P())
    return jax.shard_map(
        per_device, mesh=mesh, in_specs=placed, out_specs=P("span", "seq", None), check_vma=False
    )
```

time: 89.7 us -> 78.5 us (0.88)
  Pallas kernels: 86 us -> 74.8 us
    pallas_call x1, Pallas kernels: 86 us -> 74.8 us  [per_device(): pl.pallas_call(make_kernel(n_span, n_seq, tiles, X_SIZE), out_shape=jax.S...]
where the time goes in v2:
time: 78.5 us; the launch traced here: 78.4 us
  Pallas kernels  74.8 us (95%)
  local copies, waits for them, and re-layouts  2.82 us (4%)
    pallas_call x1, Pallas kernels, per_device(): pl.pallas_call(make_kernel(n_span, n_seq, tiles, X_SIZE), out_shape=jax.S...  74.8 us

profile of v2, /device:TPU:1, one launch (start us, length us, event | category | flops | bytes accessed | tf_op | source)
XLA Modules:
  0.0 78.4 jit_solution(16528249655262337228)
XLA Ops:
  0.0 0.0 copy-start
  0.7 1.5 %copy.7 = bf16[2,40,4096]{2,1,0:T(8,128)(2,1)S(1)} copy(bf16[2,40,4096]{2,0,1:T(2,128)(2,1)} %bitcast.17) | data formatting | bytes 1310720 | tf_op jit(solution)/shard_map/transpose | solution.py:409
  2.2 0.0 copy-start.1
  2.2 0.0 copy-done
  2.2 0.6 copy-done.1
  2.9 74.8 %span_attention.1 = bf16[5,8,4096]{2,1,0:T(8,128)(2,1)S(1)} custom-call(s32[1,128]{1,0:T(1,128)S(1)} %bitcast.16, s32[1]{0:T(128)S(6)} %copy.9.id_ref, bf16[2,5,8,4096]{3,2,1,0:T(8,128)(2,1)S(1)} %bitcast.13, bf16[3,5,8,4096]{3,2,1,0:T(8,128)(2,1)S(1)} %bitcast.15), custom_call_target="tpu_custom_call" | custom-call | flops 6710886400 | bytes 2097152 | tf_op jit(solution)/shard_map/span_attention/pallas_call | solution.py:413
  77.6 0.7 copy.10
Async XLA Ops:
  0.0 2.2 %copy-start = (bf16[1,40,3,4096]{3,1,2,0:T(8,128)(2,1)S(1)}, bf16[1,40,3,4096]{3,1,2,0:T(8,128)(2,1)}, u32[]{:S(2)}) copy-start(bf16[1,40,3,4096]{3,1,2,0:T(8,128)(2,1)} %param.4) | copy-start | bytes 2949124
  2.2 0.7 copy-start.1

commit v3 on v2

--- a/solution.py
+++ b/solution.py
@@ -257,30 +257,31 @@
 
             @pl.when(i == 3)
             def _():
-                scattered(kv.at[0, y], 1, 0, 1)
-                pass_on(0, y, 1, above)
-                pass_on(0, y, 1, below)
+                for kind in range(2):
+                    scattered(kv.at[kind, y], 1, kind, 1)
+                    pass_on(kind, y, 1, above)
+                    pass_on(kind, y, 1, below)
                 for group in range(2):
                     scatter(noisy_ref.at[1], kv.at[0, near], 1, 3, group)
                 queries_across.wait_recv()
 
+            @pl.when(i == 4)
+            def _():
+                arrived(0, below, 1)
+                pass_on(0, below, 1, above)
+
             @pl.when(i == 6)
             def _():
-                scattered(kv.at[1, y], 1, 1, 1)
-                pass_on(1, y, 1, above)
-                pass_on(1, y, 1, below)
+                arrived(1, above, 1)
+                pass_on(1, above, 1, below)
+
+            @pl.when(i == 7)
+            def _():
                 for group in range(2):
                     scatter(noisy_ref.at[2], kv.at[1, near], 1, 4, group)
 
-            @pl.when(i == 7)
-            def _():
-                arrived(0, below, 1)
-                pass_on(0, below, 1, above)
-
             @pl.when(i == 8)
             def _():
-                arrived(1, above, 1)
-                pass_on(1, above, 1, below)
                 arrived(0, above, 1)
 
             @pl.when(i == 9)
@@ -299,6 +300,12 @@
         arrived(0, opposite, 1)
         arrived(1, opposite, 1)
         loosen(opposite, 1, half, half_unit)
+
+        backward = tuple(reversed(range(n_chunk)))
+
+        def send_part(c):
+            parts_across[c].start()
+            stats_across[c].start()
 
         def give_part(c):
             part_out[rows_of(c)] = a_s[1, rows_of(c)].astype(BF16)
@@ -308,13 +315,20 @@
                     stat_out[c, pl.ds(place + b, 1)] = jnp.sum(
                         jnp.where(diagonal, stat[1, rows], 0.0), axis=0, keepdims=True
                     )
-            parts_across[c].start()
-            stats_across[c].start()
-
-        backward = tuple(reversed(range(n_chunk)))
+            if c == backward[0]:
+                send_part(c)
+            if c == backward[-1]:
+                send_part(backward[1])
+
         absorb(1, 2, opposite, 1, backward, give_part)
 
         def own_step(i, carry):
+            for place in range(2, n_chunk):
+
+                @pl.when(i == 10 + place)
+                def _(place=place):
+                    send_part(backward[place])
+
             absorb(0, 0, pick(i, 1), 1, tuple(range(n_chunk)), lambda c: None)
             return carry
 

time: 78.5 us -> 73.9 us (0.941)
  Pallas kernels: 74.8 us -> 70.2 us
    pallas_call x1, Pallas kernels: 74.8 us -> 70.2 us  [per_device(): pl.pallas_call(make_kernel(n_span, n_seq, tiles, X_SIZE), out_shape=jax.S...]
where the time goes in v3:
time: 73.9 us; the launch traced here: 73.8 us
  Pallas kernels  70.2 us (95%)
  local copies, waits for them, and re-layouts  2.82 us (4%)
  between operations  0.76 us (1%)
    pallas_call x1, Pallas kernels, per_device(): pl.pallas_call(make_kernel(n_span, n_seq, tiles, X_SIZE), out_shape=jax.S...  70.2 us

profile of v3, /device:TPU:1, one launch (start us, length us, event | category | flops | bytes accessed | tf_op | source)
XLA Modules:
  0.0 73.8 jit_solution(2297245497757396848)
XLA Ops:
  0.0 0.0 copy-start
  0.7 1.5 %copy.7 = bf16[2,40,4096]{2,1,0:T(8,128)(2,1)S(1)} copy(bf16[2,40,4096]{2,0,1:T(2,128)(2,1)} %bitcast.17) | data formatting | bytes 1310720 | tf_op jit(solution)/shard_map/transpose | solution.py:423
  2.2 0.0 copy-start.1
  2.2 0.0 copy-done
  2.2 0.6 copy-done.1
  2.9 70.2 %span_attention.1 = bf16[5,8,4096]{2,1,0:T(8,128)(2,1)S(1)} custom-call(s32[1,128]{1,0:T(1,128)S(1)} %bitcast.16, s32[1]{0:T(128)S(6)} %copy.9.id_ref, bf16[2,5,8,4096]{3,2,1,0:T(8,128)(2,1)S(1)} %bitcast.13, bf16[3,5,8,4096]{3,2,1,0:T(8,128)(2,1)S(1)} %bitcast.15), custom_call_target="tpu_custom_call" | custom-call | flops 6710886400 | bytes 2097152 | tf_op jit(solution)/shard_map/span_attention/pallas_call | solution.py:427
  73.1 0.7 copy.10
Async XLA Ops:
  0.0 2.2 %copy-start = (bf16[1,40,3,4096]{3,1,2,0:T(8,128)(2,1)S(1)}, bf16[1,40,3,4096]{3,1,2,0:T(8,128)(2,1)}, u32[]{:S(2)}) copy-start(bf16[1,40,3,4096]{3,1,2,0:T(8,128)(2,1)} %param.4) | copy-start | bytes 2949124
  2.2 0.7 copy-start.1

commit v4 on v3

--- a/solution.py
+++ b/solution.py
@@ -110,6 +110,29 @@
         def scattered(dst, first, which, group):
             whole = dst.at[pl.ds(first + group * half_unit, half_unit)]
             pltpu.make_async_copy(whole, whole, in_recv.at[which, group]).wait()
+
+        def scatter_pair(group):
+            for distance, base in routes[group]:
+                here = kv.at[:, near, slab(1, base + corner)]
+
+                def send(p, carry, distance=distance, here=here):
+                    t = seat(distance, lax.rem(corner + p, 4))
+                    pltpu.make_async_remote_copy(
+                        src_ref=noisy_ref.at[pl.ds(1, 2), :, :, columns(t)],
+                        dst_ref=here,
+                        send_sem=in_send.at[3, group],
+                        recv_sem=in_recv.at[3, group],
+                        device_id=(span, t),
+                    ).start()
+                    return carry
+
+                if group == 0 and base == 0:
+                    lax.fori_loop(1, 4, send, 0)
+                    pltpu.make_async_copy(
+                        noisy_ref.at[pl.ds(1, 2), :, :, columns(seq)], here, in_recv.at[3, group]
+                    ).start()
+                else:
+                    lax.fori_loop(0, 4, send, 0)
 
         def unit_of(kind, j, group):
             if group == 0:
@@ -262,7 +285,7 @@
                     pass_on(kind, y, 1, above)
                     pass_on(kind, y, 1, below)
                 for group in range(2):
-                    scatter(noisy_ref.at[1], kv.at[0, near], 1, 3, group)
+                    scatter_pair(group)
                 queries_across.wait_recv()
 
             @pl.when(i == 4)
@@ -274,11 +297,6 @@
             def _():
                 arrived(1, above, 1)
                 pass_on(1, above, 1, below)
-
-            @pl.when(i == 7)
-            def _():
-                for group in range(2):
-                    scatter(noisy_ref.at[2], kv.at[1, near], 1, 4, group)
 
             @pl.when(i == 8)
             def _():
@@ -334,9 +352,10 @@
 
         lax.fori_loop(11, len(plan), own_step, 0)
 
-        for which in (3, 4):
-            for group in range(2):
-                scattered(kv.at[which - 3, near], 1, which, group)
+        pair = kv.at[:, near, pl.ds(1, unit)]
+        for group in range(2):
+            some = pair.at[:, pl.ds(group * half_unit, half_unit)]
+            pltpu.make_async_copy(some, some, in_recv.at[3, group]).wait()
         loosen(near, 0, tokens, unit)
         place = out_ref.at[:, :, columns(seq)]
 
@@ -384,13 +403,17 @@
             outbuf[pl.ds(c * per_chunk * tiles, per_chunk * tiles)] = (
                 result.reshape(per_chunk * tiles, ROW, HD).astype(BF16)
             )
-            for g in reversed(range(2 * c, 2 * c + 2)):
-                for p in range(4):
-                    if g > 0:
-                        give(4 * g + p, seat(back[g][p % 2], p))
-                    elif p > 0:
-                        other = lax.rem(corner + p, 4)
-                        give(other, seat(0, other))
+
+            @pl.when(seq >= 0)
+            def _(c=c):
+                for g in reversed(range(2 * c, 2 * c + 2)):
+                    for p in range(4):
+                        if g > 0:
+                            give(4 * g + p, seat(back[g][p % 2], p))
+                        elif p > 0:
+                            other = lax.rem(corner + p, 4)
+                            give(other, seat(0, other))
+
         own_copy = pltpu.make_async_copy(outbuf.at[slab(0, corner)], place, out_recv)
         own_copy.start()
 
@@ -398,9 +421,12 @@
             some = outbuf.at[pl.ds(0, count * tiles)]
             pltpu.make_async_copy(some, some, sem).wait()
 
-        for which in range(5):
+        for which in range(3):
             drained(n_seq // 2 - 1, in_send.at[which, 0])
             drained(n_seq // 2, in_send.at[which, 1])
+        for group in range(2):
+            some = kv.at[:, near, pl.ds(1, (n_seq // 2 - 1 + group) * tiles)]
+            pltpu.make_async_copy(some, some, in_send.at[3, group]).wait()
         for slot, (kind, j, group) in enumerate(ring_sent):
             whole = unit_of(kind, j, group)
             pltpu.make_async_copy(whole, whole, ring_send.at[slot]).wait()
@@ -443,7 +469,7 @@
             pltpu.VMEM((N_CHUNK, 2 * ROW, HD), F32),
             pltpu.VMEM((N_CHUNK, 2 * ROW, HD), F32),
             pltpu.VMEM((unit, ROW, HD), BF16),
-            dma((5, 2)), dma((5, 2)), dma((12,)), dma((2, ring, 2)),
+            dma((4, 2)), dma((4, 2)), dma((12,)), dma((2, ring, 2)),
             dma((2 * N_CHUNK + 1,)), dma((2 * N_CHUNK + 1,)), dma, dma,
         ],
         compiler_params=pltpu.CompilerParams(

time: 73.9 us -> 73.5 us (level)
  no operation moved by 1% of the time
where the time goes in v4:
time: 73.5 us; the launch traced here: 73.3 us
  Pallas kernels  69.7 us (95%)
  local copies, waits for them, and re-layouts  2.82 us (4%)
  between operations  0.76 us (1%)
    pallas_call x1, Pallas kernels, per_device(): pl.pallas_call(make_kernel(n_span, n_seq, tiles, X_SIZE), out_shape=jax.S...  69.7 us

profile of v4, /device:TPU:1, one launch (start us, length us, event | category | flops | bytes accessed | tf_op | source)
XLA Modules:
  0.0 73.3 jit_solution(4688535133598578546)
XLA Ops:
  0.0 0.0 copy-start
  0.7 1.5 %copy.7 = bf16[2,40,4096]{2,1,0:T(8,128)(2,1)S(1)} copy(bf16[2,40,4096]{2,0,1:T(2,128)(2,1)} %bitcast.17) | data formatting | bytes 1310720 | tf_op jit(solution)/shard_map/transpose | solution.py:449
  2.2 0.0 copy-start.1
  2.2 0.0 copy-done
  2.2 0.6 copy-done.1
  2.9 69.7 %span_attention.1 = bf16[5,8,4096]{2,1,0:T(8,128)(2,1)S(1)} custom-call(s32[1,128]{1,0:T(1,128)S(1)} %bitcast.16, s32[1]{0:T(128)S(6)} %copy.9.id_ref, bf16[2,5,8,4096]{3,2,1,0:T(8,128)(2,1)S(1)} %bitcast.13, bf16[3,5,8,4096]{3,2,1,0:T(8,128)(2,1)S(1)} %bitcast.15), custom_call_target="tpu_custom_call" | custom-call | flops 6710886400 | bytes 2097152 | tf_op jit(solution)/shard_map/span_attention/pallas_call | solution.py:453
  72.6 0.7 copy.10
Async XLA Ops:
  0.0 2.2 %copy-start = (bf16[1,40,3,4096]{3,1,2,0:T(8,128)(2,1)S(1)}, bf16[1,40,3,4096]{3,1,2,0:T(8,128)(2,1)}, u32[]{:S(2)}) copy-start(bf16[1,40,3,4096]{3,1,2,0:T(8,128)(2,1)} %param.4) | copy-start | bytes 2949124
  2.2 0.7 copy-start.1
